TPU v7x, 32 devices: a whole 2x2x4 slice. The times are simulated.
32 devices in a mesh: table: 4 (over y, x), blk: 8 (over z, core).
Axes of the slice: x: 2, y: 2, z: 4, core: 2. Of those that a mesh axis runs over, the one named last changes fastest.
Arguments:
- cold_table: bfloat16 [131072, 128], P('table'), may hold values from -6 to 6
- slot_row: int32 [128, 2048], P(('table', 'blk')), may hold values from 0 to 32767
- slot_sample: int32 [128, 2048], P(('table', 'blk')), may hold values from 0 to 511
- slot_count: int32 [128, 2048], P(('table', 'blk')), may hold values from 0 to 15, as said below
- hot_table: bfloat16 [2048, 128], replicated, may hold values from -6 to 6
- hot_index: int32 [16384, 8], P(('table', 'blk')), may hold values from 0 to 2047
- hot_count: int32 [16384, 8], P(('table', 'blk')), may hold values from 1 to 15
- hot_cotangent: bfloat16 [16384, 128], P(('table', 'blk')), may hold values from -0.59765625 to 0.59765625
Outputs:
- features: bfloat16 [16384, 256], P(('table', 'blk'))
- hot_grad: float32 [2048, 128], P('blk')
Inputs may be any that keep to these rules, and one draw needn't show every extreme that they name: `slot_count`: slots of a bucket that carry no request have count 0 and follow its used slots; in every draw, for every index of blk, one cold shard receives 2048 used slots from every device with that index.
All inputs are finite; a program needn't handle non-finite values.
Results may differ from a plain program's by a relative error of at most 0.001.
Values may be sent and summed in bfloat16 or wider, within the bound.
A program may use at most 128 MiB of HBM per device.

v0:
```python
import jax
import jax.numpy as jnp
from jax import lax
from jax.sharding import PartitionSpec as P

cold_scale = 0.03125
hot_scale = 0.0625


def incidence_pool(sample_idx, counts, picked, samples):
    matches = jnp.arange(samples, dtype=jnp.int32)[:, None] == sample_idx[None, :]
    weights = jnp.where(matches, counts[None, :].astype(jnp.float32) * cold_scale, 0.0).astype(
        jnp.bfloat16
    )
    return jnp.dot(weights, picked, preferred_element_type=jnp.float32)


def hot_incidence(hot_index, hot_count, hot_rows):
    row_ids = jnp.arange(hot_rows, dtype=jnp.int32)[None, :]
    hot_weights = hot_count.astype(jnp.float32) * hot_scale
    lookups = hot_index.shape[1]

    def add_lookup(step, total):
        index_col = lax.dynamic_slice_in_dim(hot_index, step, 1, 1)
        weight_col = lax.dynamic_slice_in_dim(hot_weights, step, 1, 1)
        return total + jnp.where(index_col == row_ids, weight_col, 0.0)

    empty = jnp.zeros((hot_index.shape[0], hot_rows), jnp.float32)
    return lax.fori_loop(0, lookups, add_lookup, empty).astype(jnp.bfloat16)


def shards(
    cold_table, slot_row, slot_sample, slot_count, hot_table, hot_index, hot_count, hot_cotangent
):
    samples = hot_index.shape[0]
    width = cold_table.shape[1]
    got_row = lax.all_to_all(slot_row, "table", split_axis=0, concat_axis=0, tiled=True)
    picked = jnp.take(cold_table, got_row, axis=0)
    returned = lax.all_to_all(picked, "table", split_axis=0, concat_axis=0, tiled=True)

    def add_owner(total, packed):
        return (total + incidence_pool(packed[0], packed[1], packed[2], samples), None)

    cold_pooled, _ = lax.scan(
        add_owner, jnp.zeros((samples, width), jnp.float32), (slot_sample, slot_count, returned)
    )
    hot_rows = hot_table.shape[0]
    incidence = hot_incidence(hot_index, hot_count, hot_rows)
    hot_pooled = jnp.dot(incidence, hot_table, preferred_element_type=jnp.float32)
    features = jnp.concatenate(
        [cold_pooled.astype(jnp.bfloat16), hot_pooled.astype(jnp.bfloat16)], axis=1
    )
    local_sums = lax.dot_general(
        incidence, hot_cotangent, (((0,), (0,)), ((), ())), preferred_element_type=jnp.float32
    )
    share_rows = lax.psum_scatter(local_sums, "blk", scatter_dimension=0, tiled=True)
    hot_grad = lax.psum(share_rows, "table")
    return (features, hot_grad)


def solution(mesh):
    return jax.shard_map(
        shards,
        mesh=mesh,
        in_specs=(
            P("table", None),
            P(("table", "blk"), None),
            P(("table", "blk"), None),
            P(("table", "blk"), None),
            P(),
            P(("table", "blk"), None),
            P(("table", "blk"), None),
            P(("table", "blk"), None),
        ),
        out_specs=(P(("table", "blk"), None), P("blk", None)),
        check_vma=False,
    )
```

profile of v0, /device:TPU:0, one launch (start us, length us, event | category | flops | bytes accessed | tf_op | source)
XLA Modules:
  0.0 153.9 jit_solution(17119137836158717778)
XLA Ops:
  7.2 1.5 all_to_all.13
  8.6 5.2 %all-to-all-start = ((s32[4,1,2048]{2,1,0:T(1,128)}), s32[4,1,2048]{2,1,0:T(1,128)S(1)}, u32[]{:S(2)}, u32[]{:S(2)}) async-start(s32[4,1,2048]{2,1,0:T(1,128)} %all_to_all.13), calls=%async_computation | async-start | bytes 65536 | tf_op jit(solution)/shard_map/all_to_all | solution.py:37
  14.5 42.8 %while.26 = (s32[]{:T(128)}, f32[512,2048]{1,0:T(8,128)}, s32[512,8]{0,1:T(8,128)}, f32[512,8]{0,1:T(8,128)S(1)}, s32[]{:T(128)}, /*index=5*/s32[]{:T(128)}) while((s32[]{:T(128)}, f32[512,2048]{1,0:T(8,128)}, s32[512,8]{0,1:T(8,128)}, f32[512,8]{0,1:T(8,128)S(1)}, s32[]{:T(128)}, /*index=5*/s32[]{:T(128)}) %tuple.55), condition=%wide.region_3.4_spmd.clone, body=%wide.region_2.3_spmd.clone.sunk | while | flops 4194307 | bytes 8400991 | solution.py:29
  15.3 2.7 %select_add_fusion.2 = f32[512,2048]{1,0:T(8,128)} fusion(f32[512,2048]{1,0:T(8,128)} %get-tuple-element.245, f32[512]{0:T(512)S(1)} %bitcast.30, s32[512]{0:T(512)S(1)} %bitcast.31, pred[]{:T(512)S(6)} %compare.7), kind=kLoop, calls=%fused_computation.16.clone.1 | loop fusion | flops 4194304 | bytes 8392705 | tf_op jit(solution)/shard_map/while/body/eval_jaxpr/add | solution.py:26
  18.7 4.9 %select_add_fusion.2 = f32[512,2048]{1,0:T(8,128)} fusion(f32[512,2048]{1,0:T(8,128)} %get-tuple-element.245, f32[512]{0:T(512)S(1)} %bitcast.30, s32[512]{0:T(512)S(1)} %bitcast.31, pred[]{:T(512)S(6)} %compare.7), kind=kLoop, calls=%fused_computation.16.clone.1 | loop fusion | flops 4194304 | bytes 8392705 | tf_op jit(solution)/shard_map/while/body/eval_jaxpr/add | solution.py:26
  24.4 4.9 %select_add_fusion.2 = f32[512,2048]{1,0:T(8,128)} fusion(f32[512,2048]{1,0:T(8,128)} %get-tuple-element.245, f32[512]{0:T(512)S(1)} %bitcast.30, s32[512]{0:T(512)S(1)} %bitcast.31, pred[]{:T(512)S(6)} %compare.7), kind=kLoop, calls=%fused_computation.16.clone.1 | loop fusion | flops 4194304 | bytes 8392705 | tf_op jit(solution)/shard_map/while/body/eval_jaxpr/add | solution.py:26
  30.0 4.9 %select_add_fusion.2 = f32[512,2048]{1,0:T(8,128)} fusion(f32[512,2048]{1,0:T(8,128)} %get-tuple-element.245, f32[512]{0:T(512)S(1)} %bitcast.30, s32[512]{0:T(512)S(1)} %bitcast.31, pred[]{:T(512)S(6)} %compare.7), kind=kLoop, calls=%fused_computation.16.clone.1 | loop fusion | flops 4194304 | bytes 8392705 | tf_op jit(solution)/shard_map/while/body/eval_jaxpr/add | solution.py:26
  35.6 4.9 %select_add_fusion.2 = f32[512,2048]{1,0:T(8,128)} fusion(f32[512,2048]{1,0:T(8,128)} %get-tuple-element.245, f32[512]{0:T(512)S(1)} %bitcast.30, s32[512]{0:T(512)S(1)} %bitcast.31, pred[]{:T(512)S(6)} %compare.7), kind=kLoop, calls=%fused_computation.16.clone.1 | loop fusion | flops 4194304 | bytes 8392705 | tf_op jit(solution)/shard_map/while/body/eval_jaxpr/add | solution.py:26
  41.2 4.9 %select_add_fusion.2 = f32[512,2048]{1,0:T(8,128)} fusion(f32[512,2048]{1,0:T(8,128)} %get-tuple-element.245, f32[512]{0:T(512)S(1)} %bitcast.30, s32[512]{0:T(512)S(1)} %bitcast.31, pred[]{:T(512)S(6)} %compare.7), kind=kLoop, calls=%fused_computation.16.clone.1 | loop fusion | flops 4194304 | bytes 8392705 | tf_op jit(solution)/shard_map/while/body/eval_jaxpr/add | solution.py:26
  46.8 4.9 %select_add_fusion.2 = f32[512,2048]{1,0:T(8,128)} fusion(f32[512,2048]{1,0:T(8,128)} %get-tuple-element.245, f32[512]{0:T(512)S(1)} %bitcast.30, s32[512]{0:T(512)S(1)} %bitcast.31, pred[]{:T(512)S(6)} %compare.7), kind=kLoop, calls=%fused_computation.16.clone.1 | loop fusion | flops 4194304 | bytes 8392705 | tf_op jit(solution)/shard_map/while/body/eval_jaxpr/add | solution.py:26
  52.5 4.9 %select_add_fusion.2 = f32[512,2048]{1,0:T(8,128)} fusion(f32[512,2048]{1,0:T(8,128)} %get-tuple-element.245, f32[512]{0:T(512)S(1)} %bitcast.30, s32[512]{0:T(512)S(1)} %bitcast.31, pred[]{:T(512)S(6)} %compare.7), kind=kLoop, calls=%fused_computation.16.clone.1 | loop fusion | flops 4194304 | bytes 8392705 | tf_op jit(solution)/shard_map/while/body/eval_jaxpr/add | solution.py:26
  57.3 3.9 %fusion.11 = f32[2048,128]{1,0:T(8,128)} fusion(bf16[512,128]{1,0:T(8,128)(2,1)S(1)} %copy-done.1, f32[512,2048]{1,0:T(8,128)} %get-tuple-element.124), kind=kOutput, calls=%fused_computation.21 | convolution fusion | flops 269484032 | bytes 5373952 | tf_op jit(solution)/shard_map/dot_general | solution.py:53
  61.4 26.4 %gather_fusion = bf16[8192,128]{1,0:T(8,128)(2,1)S(1)} fusion(bf16[32768,128]{1,0:T(8,128)(2,1)} %param.12, s32[8192]{0:T(1024)S(1)} %broadcast_clamp_fusion), kind=kCustom, calls=%fused_computation | custom fusion | bytes 4227072 | tf_op jit(solution)/shard_map/jit(_take)/gather | solution.py:38
  87.8 3.6 %broadcast_select_fusion = bf16[4,2048,128]{2,1,0:T(8,128)(2,1)} fusion(bf16[4,2048,128]{2,1,0:T(8,128)(2,1)S(1)} %bitcast.27, pred[4,2048]{1,0:T(4,128)(4,1)S(1)} %compare_and_fusion), kind=kLoop, calls=%fused_computation.19 | loop fusion | flops 1048576 | bytes 4202496 | tf_op jit(solution)/shard_map/jit(_take)/select_n | solution.py:38
  91.4 4.2 %all-to-all-start.1 = ((bf16[4,2048,128]{2,1,0:T(8,128)(2,1)}), bf16[4,2048,128]{2,1,0:T(8,128)(2,1)S(1)}, u32[]{:S(2)}, u32[]{:S(2)}) async-start(bf16[4,2048,128]{2,1,0:T(8,128)(2,1)} %broadcast_select_fusion), calls=%async_computation.1 | async-start | bytes 4194304 | tf_op jit(solution)/shard_map/all_to_all | solution.py:39
  95.6 3.0 %convolution_convert_fusion = bf16[512,128]{0,1:T(8,128)(2,1)S(1)} fusion(bf16[2048,128]{1,0:T(8,128)(2,1)S(1)} %copy-done, f32[512,2048]{1,0:T(8,128)} %get-tuple-element.124), kind=kOutput, calls=%fused_computation.20 | convolution fusion | flops 269549568 | bytes 4849664 | tf_op jit(solution)/shard_map/dot_general | solution.py:49
  98.7 22.3 %all-to-all-done.1 = bf16[4,2048,128]{2,1,0:T(8,128)(2,1)S(1)} async-done(((bf16[4,2048,128]{2,1,0:T(8,128)(2,1)}), bf16[4,2048,128]{2,1,0:T(8,128)(2,1)S(1)}, u32[]{:S(2)}, u32[]{:S(2)}) %all-to-all-start.1) | async-done | bytes 2097184 | tf_op jit(solution)/shard_map/all_to_all | solution.py:39
  120.9 9.4 %while.25 = (s32[]{:T(128)}, f32[512,128]{1,0:T(8,128)S(1)}, s32[4,2048]{1,0:T(4,128)}, s32[4,2048]{1,0:T(4,128)}, bf16[4,2048,128]{2,1,0:T(8,128)(2,1)S(1)}, /*index=5*/s32[]{:T(128)}, s32[]{:T(128)}) while((s32[]{:T(128)}, f32[512,128]{1,0:T(8,128)S(1)}, s32[4,2048]{1,0:T(4,128)}, s32[4,2048]{1,0:T(4,128)}, ...), condition=%wide.region_1.2_spmd.clone, body=%wide.region_0.1_spmd.clone.sunk | while | flops 270667776 | bytes 1097835 | solution.py:44
  123.3 0.8 convert_multiply_fusion.3
  125.6 0.8 convert_multiply_fusion.3
  128.0 0.8 convert_multiply_fusion.3
  130.4 0.8 copy.13
  131.3 14.3 %all-reduce.2.cloned.1.call-done = f32[256,128]{1,0:T(8,128)} async-done(((f32[256,128]{1,0:T(8,128)}), f32[256,128]{1,0:T(8,128)}) %all-reduce.2.cloned.1.call-update) | async-done | bytes 131088 | tf_op jit(solution)/shard_map/psum | solution.py:57
  145.5 1.6 %copy.31 = f32[256,128]{1,0:T(8,128)} copy(f32[256,128]{1,0:T(8,128)} %all-reduce.2.cloned.1.call-done) | data formatting | bytes 262144
  (43 shorter events, 13.8 us)
Async XLA Ops:
  7.2 88.4 %copy-start = (bf16[2048,128]{1,0:T(8,128)(2,1)S(1)}, bf16[2048,128]{1,0:T(8,128)(2,1)}, u32[]{:S(2)}) copy-start(bf16[2048,128]{1,0:T(8,128)(2,1)} %param.16) | copy-start | bytes 1572868
  8.6 52.7 %all-to-all-start = ((s32[4,1,2048]{2,1,0:T(1,128)}), s32[4,1,2048]{2,1,0:T(1,128)S(1)}, u32[]{:S(2)}, u32[]{:S(2)}) async-start(s32[4,1,2048]{2,1,0:T(1,128)} %all_to_all.13), calls=%async_computation | async-start | bytes 65536 | tf_op jit(solution)/shard_map/all_to_all | solution.py:37
  13.8 84.8 %reduce-scatter.2.cloned.1.call-start = ((), (), s32[]{:S(2)}) async-start(), calls=%async_computation.3 | async-start | bytes 1179648 | tf_op jit(solution)/shard_map/reduce_scatter | solution.py:56
  14.5 42.8 %copy-start.1 = (bf16[512,128]{1,0:T(8,128)(2,1)S(1)}, bf16[512,128]{1,0:T(8,128)(2,1)}, u32[]{:S(2)}) copy-start(bf16[512,128]{1,0:T(8,128)(2,1)} %param.19) | copy-start | bytes 393220
  91.4 29.6 %all-to-all-start.1 = ((bf16[4,2048,128]{2,1,0:T(8,128)(2,1)}), bf16[4,2048,128]{2,1,0:T(8,128)(2,1)S(1)}, u32[]{:S(2)}, u32[]{:S(2)}) async-start(bf16[4,2048,128]{2,1,0:T(8,128)(2,1)} %broadcast_select_fusion), calls=%async_computation.1 | async-start | bytes 4194304 | tf_op jit(solution)/shard_map/all_to_all | solution.py:39
  95.6 50.0 %all-reduce.2.cloned.1.call-start = ((), (), s32[]{:S(2)}) async-start(), calls=%async_computation.4 | async-start | bytes 262144 | tf_op jit(solution)/shard_map/psum | solution.py:57
Sparse Core Ops, SparseCore 0:
  61.4 34.0 reduce-scatter.1
  99.3 46.1 all-reduce.1
where the time goes:
time: 156 us; the launch traced here: 154 us
  other arithmetic  44.5 us (29%)
  local copies, waits for them, and re-layouts  39.3 us (25%)
  waiting for transfers between devices  36.6 us (23%)
  between operations  14.1 us (9%)
  matrix products  10 us (6%)
  starting transfers between devices  9.37 us (6%)
    add x8, other arithmetic, add_lookup(): return total + jnp.where(index_col == row_ids, weight_col, 0.0)  36.9 us
    gather x1, local copies, waits for them, and re-layouts, shards(): picked = jnp.take(cold_table, got_row, axis=0)  26.4 us
    all_to_all x1, waiting for transfers between devices, shards(): lax.all_to_all(picked, 'table', split_axis=0, concat_axis=0, tiled=True)  22.3 us
    psum x1, waiting for transfers between devices, shards(): hot_grad = lax.psum(share_rows, 'table')  14.3 us
    dynamic_slice x8, local copies, waits for them, and re-layouts, add_lookup(): index_col = lax.dynamic_slice_in_dim(hot_index, step, 1, 1)  5.82 us
    all_to_all x1, starting transfers between devices, shards(): lax.all_to_all(slot_row, 'table', split_axis=0, concat_axis=0, tiled=True)  5.16 us
    all_to_all x1, starting transfers between devices, shards(): lax.all_to_all(picked, 'table', split_axis=0, concat_axis=0, tiled=True)  4.2 us
    dot_general x1, matrix products, shards(): lax.dot_general(incidence, hot_cotangent, (((0,), (0,)), ((), ())), prefe...  3.92 us
  transfers between devices with their start and end apart: 4, of which 2 were waited for; matrix products, arithmetic and copies ran while one was open for 59% of the time, Pallas kernels for 0%

commit v1 on v0

v1 whole, which is shorter than its diff:
```python
import functools

import jax
import jax.numpy as jnp
from jax import lax
from jax.experimental import pallas as pl
from jax.experimental.pallas import tpu as pltpu
from jax.sharding import PartitionSpec as P

MESH = pl.DeviceIdType.MESH
cold_scale = 0.03125
hot_scale = 0.0625
LANES = 128
TABLE_CHUNKS = 8
GROUP = 32


def kernel(
    tables,
    blks,
    table_hbm,
    req_ref,
    hot_ref,
    index_ref,
    count_ref,
    cot_ref,
    feat_ref,
    grad_ref,
    staged,
    wide,
    req_in,
    rows_smem,
    inc,
    grad_all,
    core_in,
    halves,
    table_in,
    quarter,
    z_in,
    gathered,
    weights,
    pooled,
    pooled_in,
    total,
    shares,
    stage_sem,
    smem_sem,
    req_send,
    req_recv,
    core_sem,
    tab_send,
    tab_recv,
    z_send,
    z_recv,
    ag_send,
    ag_recv,
    pool_send,
    pool_recv,
):
    me_t = lax.axis_index("table")
    me_b = lax.axis_index("blk")
    core = lax.rem(me_b, 2)
    me_z = me_b // 2
    zs = blks // 2
    samples = cot_ref.shape[0]
    hot_rows = hot_ref.shape[0]
    block = hot_rows // blks
    share = block // tables
    req_rows = req_ref.shape[2]
    chunk = table_hbm.shape[0] // TABLE_CHUNKS

    stage_copies = []
    for i in range(TABLE_CHUNKS):
        part = pl.ds(i * chunk, chunk)
        copy = pltpu.make_async_copy(table_hbm.at[part], staged.at[part], stage_sem.at[i])
        copy.start()
        stage_copies.append(copy)

    def table_peer(k):
        return (lax.rem(me_t + k, tables), me_b)

    def z_peer(k):
        return (me_t, lax.rem(me_z + k, zs) * 2 + core)

    core_peer = (me_t, me_z * 2 + 1 - core)
    partners = [table_peer(k) for k in range(1, tables)]
    partners += [z_peer(k) for k in range(1, zs)] + [core_peer]
    barrier = pltpu.get_barrier_semaphore()
    for partner in partners:
        pl.semaphore_signal(barrier, inc=1, device_id=partner, device_id_type=MESH)
    pl.semaphore_wait(barrier, len(partners))

    def send(src, dst, send_sem, recv_sem, to):
        copy = pltpu.make_async_remote_copy(
            src_ref=src,
            dst_ref=dst,
            send_sem=send_sem,
            recv_sem=recv_sem,
            device_id=to,
            device_id_type=MESH,
        )
        copy.start()
        return copy

    req_copies = [
        send(
            req_ref.at[lax.rem(me_t + k, tables)],
            req_in.at[k - 1],
            req_send.at[k - 1],
            req_recv.at[k - 1],
            table_peer(k),
        )
        for k in range(1, tables)
    ]

    tile = 64
    for lane in range(samples // LANES):
        cols = pl.ds(lane * LANES, LANES)
        lookups = index_ref.shape[0]
        idx = [index_ref[k : k + 1, cols] for k in range(lookups)]
        wts = [count_ref[k : k + 1, cols].astype(jnp.float32) * hot_scale for k in range(lookups)]
        ids = lax.broadcasted_iota(jnp.int32, (tile, LANES), 0)

        def add_tile(r, carry):
            base = pl.multiple_of(r * tile, tile)
            here = ids + base
            acc = jnp.where(here == idx[0], wts[0], 0.0)
            for k in range(1, lookups):
                acc = acc + jnp.where(here == idx[k], wts[k], 0.0)
            inc[pl.ds(base, tile), cols] = acc.astype(jnp.bfloat16)
            return carry

        lax.fori_loop(0, hot_rows // tile, add_tile, 0)

    def grad_block(b, carry):
        base = pl.multiple_of(b * block, block)
        grad_all[lax.rem(b, 2), b // 2] = jnp.dot(
            inc[pl.ds(base, block), :], cot_ref[...], preferred_element_type=jnp.float32
        )
        return carry

    lax.fori_loop(0, blks, grad_block, 0)
    core_copy = send(grad_all.at[1 - core], core_in, core_sem.at[0], core_sem.at[1], core_peer)

    hot_t = lax.dot_general(
        hot_ref[...], inc[...], (((0,), (0,)), ((), ())), preferred_element_type=jnp.float32
    )
    width = hot_ref.shape[1]
    feat_ref[:, width:] = hot_t.T.astype(jnp.bfloat16)

    own_copy = pltpu.make_async_copy(req_ref.at[me_t, 0], rows_smem.at[tables - 1], smem_sem.at[tables - 1])
    own_copy.start()
    smem_copies = []
    for k in range(1, tables):
        req_copies[k - 1].wait()
        copy = pltpu.make_async_copy(req_in.at[k - 1, 0], rows_smem.at[k - 1], smem_sem.at[k - 1])
        copy.start()
        smem_copies.append(copy)
    smem_copies.append(own_copy)

    step = 256
    for i in range(TABLE_CHUNKS):
        stage_copies[i].wait()

        def widen(r, carry):
            part = pl.ds(pl.multiple_of(i * chunk + r * step, step), step)
            wide[part, :] = staged[part, :].astype(jnp.float32)
            return carry

        lax.fori_loop(0, chunk // step, widen, 0)
    for copy in smem_copies:
        copy.wait()

    def pool(slot, load_meta):
        def body(i, carry):
            base = pl.multiple_of(i * LANES, LANES)
            sample = load_meta(1, i)
            weight = load_meta(2, i).astype(jnp.float32) * cold_scale
            for s in range(samples // LANES):
                ids = lax.broadcasted_iota(jnp.int32, (LANES, LANES), 0) + s * LANES
                weights[pl.ds(s * LANES, LANES), pl.ds(base, LANES)] = jnp.where(
                    ids == sample, weight, 0.0
                ).astype(jnp.bfloat16)
            for g in range(0, LANES, GROUP):
                got = [wide[pl.ds(rows_smem[slot, i, g + j], 1), :] for j in range(GROUP)]
                for j in range(GROUP):
                    gathered[pl.ds(base + g + j, 1), :] = got[j]
            return carry

        lax.fori_loop(0, req_rows, body, 0)
        return jnp.dot(
            weights[...], gathered[...].astype(jnp.bfloat16), preferred_element_type=jnp.float32
        )

    def pool_peer(k):
        pooled[k - 1] = pool(k - 1, lambda f, i: req_in[k - 1, f, pl.ds(i, 1), :])
        return send(
            pooled.at[k - 1],
            pooled_in.at[k - 1],
            pool_send.at[k - 1],
            pool_recv.at[k - 1],
            (lax.rem(me_t + tables - k, tables), me_b),
        )

    def core_stage():
        core_copy.wait()
        for part in range(tables):
            rows = pl.ds(part * share, share)
            halves[part] = grad_all[core, :, rows, :] + core_in[:, rows, :]
        return [
            send(
                halves.at[lax.rem(me_t + k, tables)],
                table_in.at[k - 1],
                tab_send.at[k - 1],
                tab_recv.at[k - 1],
                table_peer(k),
            )
            for k in range(1, tables)
        ]

    def table_stage(copies):
        for copy in copies:
            copy.wait()
        acc = halves[me_t]
        for k in range(1, tables):
            acc = acc + table_in[k - 1]
        quarter[...] = acc
        return [
            send(
                quarter.at[lax.rem(me_z + k, zs)],
                z_in.at[k - 1],
                z_send.at[k - 1],
                z_recv.at[k - 1],
                z_peer(k),
            )
            for k in range(1, zs)
        ]

    def z_stage(copies):
        for copy in copies:
            copy.wait()
        acc = quarter[me_z]
        for k in range(1, zs):
            acc = acc + z_in[k - 1]
        total[...] = acc
        return [
            send(total, shares.at[k - 1], ag_send.at[k - 1], ag_recv.at[k - 1], table_peer(k))
            for k in range(1, tables)
        ]

    def gather_stage(copies):
        for copy in copies:
            copy.wait()
        grad_ref[pl.ds(pl.multiple_of(me_t * share, share), share), :] = total[...]
        for k in range(1, tables):
            source = lax.rem(me_t + tables - k, tables)
            grad_ref[pl.ds(pl.multiple_of(source * share, share), share), :] = shares[k - 1]

    pool_copies = []
    state = core_stage()
    stages = [table_stage, z_stage, gather_stage]
    for k in range(1, tables):
        pool_copies.append(pool_peer(k))
        if k - 1 < len(stages):
            state = stages[k - 1](state)
    cold = pool(tables - 1, lambda f, i: req_ref[me_t, f, pl.ds(i, 1), :])
    for copy in pool_copies:
        copy.wait()
    for k in range(1, tables):
        cold = cold + pooled_in[k - 1]
    feat_ref[:, :width] = cold.astype(jnp.bfloat16)


def shards(
    tables,
    blks,
    cold_table,
    slot_row,
    slot_sample,
    slot_count,
    hot_table,
    hot_index,
    hot_count,
    hot_cotangent,
):
    slots = slot_row.shape[1]
    req_rows = slots // LANES
    requests = jnp.stack([slot_row, slot_sample, slot_count], axis=1).reshape(
        tables, 3, req_rows, LANES
    )
    samples, width = hot_cotangent.shape
    hot_rows = hot_table.shape[0]
    zs = blks // 2
    block = hot_rows // blks
    share = block // tables
    f32 = jnp.float32
    dma = pltpu.SemaphoreType.DMA
    vmem = pl.BlockSpec(memory_space=pltpu.VMEM)
    return pl.pallas_call(
        functools.partial(kernel, tables, blks),
        out_shape=(
            jax.ShapeDtypeStruct((samples, 2 * width), jnp.bfloat16),
            jax.ShapeDtypeStruct((block, width), f32),
        ),
        in_specs=[pl.BlockSpec(memory_space=pl.ANY)] + [vmem] * 5,
        out_specs=(vmem, vmem),
        scratch_shapes=[
            pltpu.VMEM(cold_table.shape, jnp.bfloat16),
            pltpu.VMEM(cold_table.shape, f32),
            pltpu.VMEM((tables - 1, 3, req_rows, LANES), jnp.int32),
            pltpu.SMEM((tables, req_rows, LANES), jnp.int32),
            pltpu.VMEM((hot_rows, samples), jnp.bfloat16),
            pltpu.VMEM((2, zs, block, width), f32),
            pltpu.VMEM((zs, block, width), f32),
            pltpu.VMEM((tables, zs, share, width), f32),
            pltpu.VMEM((tables - 1, zs, share, width), f32),
            pltpu.VMEM((zs, share, width), f32),
            pltpu.VMEM((zs - 1, share, width), f32),
            pltpu.VMEM((slots, width), f32),
            pltpu.VMEM((samples, slots), jnp.bfloat16),
            pltpu.VMEM((tables - 1, samples, width), f32),
            pltpu.VMEM((tables - 1, samples, width), f32),
            pltpu.VMEM((share, width), f32),
            pltpu.VMEM((tables - 1, share, width), f32),
            dma((TABLE_CHUNKS,)),
            dma((tables,)),
            dma((tables - 1,)),
            dma((tables - 1,)),
            dma((2,)),
            dma((tables - 1,)),
            dma((tables - 1,)),
            dma((zs - 1,)),
            dma((zs - 1,)),
            dma((tables - 1,)),
            dma((tables - 1,)),
            dma((tables - 1,)),
            dma((tables - 1,)),
        ],
        compiler_params=pltpu.CompilerParams(
            collective_id=0, has_side_effects=True, vmem_limit_bytes=56 * 1024 * 1024
        ),
    )(cold_table, requests, hot_table, hot_index.T, hot_count.T, hot_cotangent)


def solution(mesh):
    both = P(("table", "blk"), None)
    return jax.shard_map(
        functools.partial(shards, mesh.shape["table"], mesh.shape["blk"]),
        mesh=mesh,
        in_specs=(P("table", None), both, both, both, P(), both, both, both),
        out_specs=(both, P("blk", None)),
        check_vma=False,
    )
```

time: 156 us -> 50.7 us (0.33); the launches traced: 154 us -> 50.3 us
  Pallas kernels: 0 us -> 44.3 us
  other arithmetic: 44.5 us -> 0.65 us
  waiting for transfers between devices: 36.6 us -> 0 us
  local copies, waits for them, and re-layouts: 39.3 us -> 4.78 us
  between operations: 14.1 us -> 0.64 us
  matrix products: 10 us -> 0 us
  starting transfers between devices: 9.37 us -> 0 us
    pallas_call x0 -> x1, Pallas kernels: none -> 44.3 us  [shards(): pl.pallas_call(functools.partial(kernel, tables, blks), out_shape=(jax.Sh...]
    add x8 -> x0, other arithmetic: 36.9 us -> none  [add_lookup(): return total + jnp.where(index_col == row_ids, weight_col, 0.0)]
    gather x1 -> x0, local copies, waits for them, and re-layouts: 26.4 us -> none  [shards(): picked = jnp.take(cold_table, got_row, axis=0)]
    all_to_all x2 -> x0, waiting for transfers between devices: 22.3 us -> none  [the longest x1 22.3 us: shards(): lax.all_to_all(picked, 'table', split_axis=0, concat_axis=0, tiled=True)]
    psum x1 -> x0, waiting for transfers between devices: 14.3 us -> none  [shards(): hot_grad = lax.psum(share_rows, 'table')]
    dot_general x6 -> x0, matrix products: 10 us -> none  [the longest x1 3.92 us: shards(): lax.dot_general(incidence, hot_cotangent, (((0,), (0,)), ((), ())), prefe...]
    all_to_all x2 -> x0, starting transfers between devices: 9.36 us -> none  [the longest x1 5.16 us: shards(): lax.all_to_all(slot_row, 'table', split_axis=0, concat_axis=0, tiled=True)]
    dynamic_slice x20 -> x0, local copies, waits for them, and re-layouts: 8.96 us -> none  [the longest x8 5.82 us: add_lookup(): index_col = lax.dynamic_slice_in_dim(hot_index, step, 1, 1)]
  transfers between devices with their start and end apart: 4 -> 0, of which waited for: 2 -> 0; matrix products, arithmetic and copies ran while one was open for 59% -> 0% of each run, Pallas kernels for 0% -> 0%
where the time goes in v1:
time: 50.7 us; the launch traced here: 50.3 us
  Pallas kernels  44.3 us (87%)
  local copies, waits for them, and re-layouts  4.78 us (9%)
  other arithmetic  0.65 us (1%)
  between operations  0.64 us (1%)
    pallas_call x1, Pallas kernels, shards(): pl.pallas_call(functools.partial(kernel, tables, blks), out_shape=(jax.Sh...  44.3 us
    unnamed x3, local copies, waits for them, and re-layouts  4 us

profile of v1, /device:TPU:0, one launch (start us, length us, event | category | flops | bytes accessed | tf_op | source)
XLA Modules:
  0.0 50.3 jit_solution(5379557490733755069)
XLA Ops:
  0.6 0.8 %copy.16 = s32[1,4,16,128]{3,2,1,0:T(8,128)S(1)} copy(s32[1,4,16,128]{3,1,2,0:T(4,128)} %bitcast.16) | data formatting | bytes 65536
  1.4 0.8 %copy_bitcast_fusion = (s32[4,1,16,128]{3,2,1,0:T(8,128)S(1)}, s32[4,1,16,128]{3,2,1,0:T(8,128)S(1)}) fusion(s32[1,4,16,128]{3,1,2,0:T(4,128)} %bitcast.17, s32[1,4,16,128]{3,1,2,0:T(4,128)} %bitcast.18), kind=kLoop, calls=%fused_computation.1 | loop fusion | bytes 131072 | tf_op jit(solution)/shard_map/stack | solution.py:288
  2.2 0.6 %pad_add_fusion.req_ref = s32[4,3,16,128]{3,2,1,0:T(8,128)} fusion(s32[4,1,16,128]{3,2,1,0:T(8,128)S(1)} %get-tuple-element.2, s32[4,1,16,128]{3,2,1,0:T(8,128)S(1)} %get-tuple-element.3, s32[4,1,16,128]{3,2,1,0:T(8,128)S(1)} %bitcast.15), kind=kLoop, calls=%fused_computation | loop fusion | flops 49152 | bytes 196608 | tf_op jit(solution)/shard_map/stack | solution.py:288
  2.8 44.3 %shard_map.95 = (bf16[512,256]{1,0:T(8,128)(2,1)}, f32[256,128]{1,0:T(8,128)}) custom-call(bf16[32768,128]{1,0:T(8,128)(2,1)} %table_hbm.1, s32[4,3,16,128]{3,2,1,0:T(8,128)} %pad_add_fusion.req_ref, bf16[2048,128]{1,0:T(8,128)(2,1)} %hot_ref.1, s32[8,512]{1,0:T(8,128)} %bitcast.19, s32[8,512]{1,0:T(8,128)} %bitcast.20, bf16[512,128]{1,0:T(8,128)(2,1)} %cot_ref.1), custom_call_target="tpu_custom_call" | custom-call | tf_op jit(solution)/shard_map/pallas_call | solution.py:299
  47.1 1.7 %copy.19 = bf16[512,256]{1,0:T(8,128)(2,1)} copy(bf16[512,256]{1,0:T(8,128)(2,1)} %get-tuple-element.6) | data formatting | bytes 524288
  48.8 1.6 %copy.20 = f32[256,128]{1,0:T(8,128)} copy(f32[256,128]{1,0:T(8,128)} %get-tuple-element.7) | data formatting | bytes 262144
